TPU v7x, 32 devices: a whole 2x2x4 slice. The times are simulated.
32 devices in a mesh: req: 4 (over x, core), kv: 8 (over z, y).
Axes of the slice: x: 2, y: 2, z: 4, core: 2. Of those that a mesh axis runs over, the one named last changes fastest.
Arguments:
- hidden_in: bfloat16 [2048, 4096], P('req'), may hold values from -6 to 6
- ln_gains: float32 [2, 4096], replicated, may hold values from 0.1 to 1.9
- qkv_weight: bfloat16 [4096, 3, 4096], P('req', None, 'kv'), may hold values from -0.09375 to 0.09375
- dense_weight: bfloat16 [4096, 4096], P('kv', 'req'), may hold values from -0.09375 to 0.09375
- up_weight: bfloat16 [4096, 16384], P('req', 'kv'), may hold values from -0.09375 to 0.09375
- down_weight: bfloat16 [16384, 4096], P('kv', 'req'), may hold values from -0.046875 to 0.046875
- cache: bfloat16 [4, 64, 2, 32, 128, 128], P('req', 'kv'), may hold values from -200 to 200
- cached_len: int32 [8], P('req'), may hold values from 1 to 4096, as said below
- page_table: int32 [8, 32], P('req'), may hold values from 0 to 63, as said below
Outputs:
- hidden_out: float32 [2048, 4096], P('req', 'kv')
Inputs may be any that keep to these rules, and one draw needn't show every extreme that they name: `page_table`: within each group of 2 consecutive requests the entries are distinct and together name each of the group's 64 slots once. `cached_len`: some request has exactly 4096 cached tokens.
All inputs are finite; a program needn't handle non-finite values.
Results may differ from a plain program's by a relative error of at most 0.012.
The roundings to bfloat16 on the way count: a program that leaves them out, or rounds other values in their place, can miss the bound.
Values may be sent and summed in bfloat16 or wider, within the bound.
A program may use at most 192 MiB of HBM per device.

v0:
```python
import jax
import jax.numpy as jnp
from jax import lax
from jax.sharding import PartitionSpec as P

D = 4096
HEADS = 32
HD = 128
ROT = 32
PAGE = 128


def layer_norm(x, gain):
    mean = jnp.mean(x, axis=-1, keepdims=True)
    cent = x - mean
    var = jnp.mean(cent * cent, axis=-1, keepdims=True)
    return cent * lax.rsqrt(var + 1e-05) * gain


def rotate(t, pos):
    half = ROT // 2
    freq = 10000.0 ** (-(jnp.arange(half, dtype=jnp.float32) * 2.0 / ROT))
    angle = pos[:, None] * freq[None, :]
    cosine = jnp.cos(angle)[:, None, :]
    sine = jnp.sin(angle)[:, None, :]
    first = t[..., :half]
    second = t[..., half:ROT]
    return jnp.concatenate(
        [first * cosine - second * sine, second * cosine + first * sine, t[..., ROT:]], axis=-1
    )


def online_update(state, scores, live, values):
    top, total, accum = state
    masked = jnp.where(live, scores, -1e30)
    new_top = jnp.maximum(top, jnp.max(masked, axis=-1))
    weights = jnp.where(live, jnp.exp(scores - new_top[..., None]), 0.0).astype(jnp.bfloat16)
    factor = jnp.exp(top - new_top)
    total = total * factor + jnp.sum(weights.astype(jnp.float32), axis=-1)
    accum = accum * factor[..., None] + jnp.einsum(
        "hqk,hkd->hqd", weights, values, preferred_element_type=jnp.float32
    )
    return (new_top, total, accum)


def per_device(
    hidden_in,
    ln_gains,
    qkv_weight,
    dense_weight,
    up_weight,
    down_weight,
    cache,
    cached_len,
    page_table,
):
    n_kv = lax.axis_size("kv")
    me_kv = lax.axis_index("kv")
    rows = hidden_in.shape[0]
    groups_here = cached_len.shape[0]
    span_rows = rows // groups_here
    width_loc = qkv_weight.shape[2]
    heads_loc = width_loc // HD
    scale = 1.0 / HD**0.5
    x = hidden_in.astype(jnp.float32)
    h1 = layer_norm(x, ln_gains[0]).astype(jnp.bfloat16)
    h2 = layer_norm(x, ln_gains[1]).astype(jnp.bfloat16)
    qkv_piece = lax.all_gather(qkv_weight, "req", axis=0, tiled=True)
    up_piece = lax.all_gather(up_weight, "req", axis=0, tiled=True)
    count = qkv_piece.shape[0]
    qkv_acc = jnp.dot(
        h1, qkv_piece.reshape(count, 3 * width_loc), preferred_element_type=jnp.float32
    )
    up_acc = jnp.dot(h2, up_piece, preferred_element_type=jnp.float32)
    qkv = qkv_acc
    qkv = qkv.reshape(rows, 3, heads_loc, HD)
    offsets = jnp.arange(span_rows, dtype=jnp.int32)
    pos = (cached_len[:, None] + offsets[None, :]).reshape(rows).astype(jnp.float32)
    query = rotate(qkv[:, 0], pos).astype(jnp.bfloat16)
    key_new = rotate(qkv[:, 1], pos).astype(jnp.bfloat16)
    value_new = qkv[:, 2].astype(jnp.bfloat16)
    q_grp = query.reshape(groups_here, span_rows, heads_loc, HD)
    k_grp = key_new.reshape(groups_here, span_rows, heads_loc, HD)
    v_grp = value_new.reshape(groups_here, span_rows, heads_loc, HD)
    causal = offsets[None, :] <= offsets[:, None]
    s_new = jnp.einsum("gqhd,gkhd->ghqk", q_grp, k_grp, preferred_element_type=jnp.float32) * scale
    s_new = jnp.where(causal[None, None], s_new, -1e30)
    top_new = jnp.max(s_new, axis=-1)
    p_new = jnp.where(causal[None, None], jnp.exp(s_new - top_new[..., None]), 0.0).astype(
        jnp.bfloat16
    )
    total_new = jnp.sum(p_new.astype(jnp.float32), axis=-1)
    accum_new = jnp.einsum("ghqk,gkhd->ghqd", p_new, v_grp, preferred_element_type=jnp.float32)
    q_all = lax.all_gather(query.reshape(rows, width_loc), "kv", axis=1, tiled=True)
    q_all = q_all.reshape(groups_here, span_rows, HEADS, HD)
    local_cache = cache[0]
    slots_here = local_cache.shape[0]
    slot_ids = me_kv * slots_here + jnp.arange(slots_here, dtype=jnp.int32)
    match = (page_table[None, :, :] == slot_ids[:, None, None]).astype(jnp.int32)
    owner_req = jnp.sum(
        match * jnp.arange(groups_here, dtype=jnp.int32)[None, :, None], axis=(1, 2)
    )
    owner_page = jnp.sum(
        match * jnp.arange(page_table.shape[1], dtype=jnp.int32)[None, None, :], axis=(1, 2)
    )
    page_pos = jnp.arange(PAGE, dtype=jnp.int32)

    def visit(slot, state):
        tops, totals, accums = state
        req = owner_req[slot]
        page_kv = lax.dynamic_index_in_dim(local_cache, slot, 0, keepdims=False)
        q_req = lax.dynamic_index_in_dim(q_all, req, 0, keepdims=False)
        scores = (
            jnp.einsum("qhd,hkd->hqk", q_req, page_kv[0], preferred_element_type=jnp.float32)
            * scale
        )
        length = lax.dynamic_index_in_dim(cached_len, req, 0, keepdims=False)
        live = (owner_page[slot] * PAGE + page_pos < length)[None, None, :]
        part_state = (
            lax.dynamic_index_in_dim(tops, req, 0, keepdims=False),
            lax.dynamic_index_in_dim(totals, req, 0, keepdims=False),
            lax.dynamic_index_in_dim(accums, req, 0, keepdims=False),
        )
        top, total, accum = online_update(part_state, scores, live, page_kv[1])
        tops = lax.dynamic_update_index_in_dim(tops, top, req, 0)
        totals = lax.dynamic_update_index_in_dim(totals, total, req, 0)
        accums = lax.dynamic_update_index_in_dim(accums, accum, req, 0)
        return (tops, totals, accums)

    empty = (
        jnp.full((groups_here, HEADS, span_rows), -1e30, jnp.float32),
        jnp.zeros((groups_here, HEADS, span_rows), jnp.float32),
        jnp.zeros((groups_here, HEADS, span_rows, HD), jnp.float32),
    )
    tops, totals, accums = lax.fori_loop(0, slots_here, visit, empty)
    own = lax.dynamic_slice_in_dim(tops, me_kv * heads_loc, heads_loc, 1)
    with_new = lax.dynamic_update_slice_in_dim(
        tops, jnp.maximum(own, top_new), me_kv * heads_loc, 1
    )
    largest = lax.pmax(with_new, "kv")
    factor = jnp.exp(tops - largest)
    sum_acc, sum_tot = (
        lax.psum_scatter(accums * factor[..., None], "kv", scatter_dimension=1, tiled=True),
        lax.psum_scatter(totals * factor, "kv", scatter_dimension=1, tiled=True),
    )
    own_largest = lax.dynamic_slice_in_dim(largest, me_kv * heads_loc, heads_loc, 1)
    fresh = jnp.exp(top_new - own_largest)
    numer = sum_acc + accum_new * fresh[..., None]
    denom = sum_tot + total_new * fresh
    att = (numer / denom[..., None]).astype(jnp.bfloat16)
    att = jnp.transpose(att, (0, 2, 1, 3)).reshape(rows, width_loc)
    hidden = jax.nn.gelu(up_acc, approximate=False).astype(jnp.bfloat16)
    dense_piece = lax.all_gather(dense_weight, "req", axis=1, tiled=True)
    down_piece = lax.all_gather(down_weight, "req", axis=1, tiled=True)
    value = jnp.dot(att, dense_piece, preferred_element_type=jnp.float32) + jnp.dot(
        hidden, down_piece, preferred_element_type=jnp.float32
    )
    summed = lax.psum_scatter(value, "kv", scatter_dimension=1, tiled=True)
    width_out = D // n_kv
    residual = lax.dynamic_slice_in_dim(x, me_kv * width_out, width_out, 1)
    return residual + summed


def solution(mesh):
    placed = (
        P("req", None),
        P(),
        P("req", None, "kv"),
        P("kv", "req"),
        P("req", "kv"),
        P("kv", "req"),
        P("req", "kv", None, None, None, None),
        P("req"),
        P("req", None),
    )
    return jax.shard_map(
        per_device, mesh=mesh, in_specs=placed, out_specs=P("req", "kv"), check_vma=False
    )
```

profile of v0, /device:TPU:0, one launch (start us, length us, event | category | flops | bytes accessed | tf_op | source)
XLA Modules:
  0.0 1139.2 jit_solution(8009860428109597316)
XLA Ops:
  6.5 4.7 copy.46
  11.4 3.0 convert_reduce_fusion.1
  16.3 80.0 %all-gather.6.cloned.1.call-done = bf16[4096,3,512]{0,2,1:T(8,128)(2,1)} async-done(((bf16[1024,3,512]{0,2,1:T(8,128)(2,1)}), bf16[4096,3,512]{0,2,1:T(8,128)(2,1)}) %all-gather.6.cloned.1.call-update) | async-done | bytes 12582928 | tf_op jit(solution)/shard_map/all_gather | solution.py:68
  96.2 11.0 fusion.14
  115.8 2.9 fusion.30
  118.8 66.4 %all-gather.8.cloned.1.call-done = bf16[512,4096]{1,0:T(8,128)(2,1)} async-done(((bf16[512,512]{1,0:T(8,128)(2,1)}), bf16[512,4096]{1,0:T(8,128)(2,1)}) %all-gather.8.cloned.1.call-update) | async-done | bytes 4194320 | tf_op jit(solution)/shard_map/all_gather | solution.py:94
  185.1 5.4 copy.67
  190.6 4.2 broadcast_in_dim.117
  194.8 175.5 %while.18 = (s32[]{:T(128)}, f32[2,32,256]{2,1,0:T(8,128)S(1)}, f32[2,32,256]{2,1,0:T(8,128)S(1)}, f32[2,32,256,128]{3,2,1,0:T(8,128)}, s32[8]{0:T(128)S(1)}, /*...) while((s32[]{:T(128)}, f32[2,32,256]{2,1,0:T(8,128)S(1)}, ...), condition=%wide.region_7.8_spmd.clone, body=%wide.region_4.7_spmd.clone.sunk | while | flops 552632576 | bytes 88573760 | solution.py:135
  199.9 2.1 constant_dynamic-slice_fusion.4
  202.0 5.1 select_reduce_fusion.2
  207.2 2.3 constant_dynamic-slice_fusion.5
  209.4 6.4 bitcast_dynamic-update-slice_fusion.2
  221.9 2.1 constant_dynamic-slice_fusion.4
  224.0 5.1 select_reduce_fusion.2
  229.1 2.3 constant_dynamic-slice_fusion.5
  231.4 6.3 bitcast_dynamic-update-slice_fusion.2
  245.9 5.1 select_reduce_fusion.2
  251.0 2.3 constant_dynamic-slice_fusion.5
  253.3 6.3 bitcast_dynamic-update-slice_fusion.2
  267.8 5.1 select_reduce_fusion.2
  273.0 2.3 constant_dynamic-slice_fusion.5
  275.2 6.4 bitcast_dynamic-update-slice_fusion.2
  289.8 5.1 select_reduce_fusion.2
  294.9 2.3 constant_dynamic-slice_fusion.5
  297.2 6.4 bitcast_dynamic-update-slice_fusion.2
  311.7 5.1 select_reduce_fusion.2
  316.8 2.3 constant_dynamic-slice_fusion.5
  319.1 6.3 bitcast_dynamic-update-slice_fusion.2
  333.6 5.1 select_reduce_fusion.2
  338.8 2.3 constant_dynamic-slice_fusion.5
  341.0 6.4 bitcast_dynamic-update-slice_fusion.2
  355.6 5.1 select_reduce_fusion.2
  360.7 2.3 constant_dynamic-slice_fusion.5
  363.0 6.3 bitcast_dynamic-update-slice_fusion.2
  371.6 66.3 %all-reduce.6.cloned.1.call-done = f32[2,32,256]{2,1,0:T(8,128)} async-done(((f32[2,32,256]{2,1,0:T(8,128)}), f32[2,32,256]{2,1,0:T(8,128)}) %all-reduce.6.cloned.1.call-update) | async-done | bytes 65552 | tf_op jit(solution)/shard_map/pmax | solution.py:140
  439.4 8.1 broadcast_multiply_fusion
  452.7 92.6 %all-gather.12.cloned.1.call-done = bf16[4096,2048]{1,0:T(8,128)(2,1)} async-done(((bf16[1024,2048]{1,0:T(8,128)(2,1)}), bf16[4096,2048]{1,0:T(8,128)(2,1)}) %all-gather.12.cloned.1.call-update) | async-done | bytes 16777232 | tf_op jit(solution)/shard_map/all_gather | solution.py:69
  545.3 23.2 %fusion.12 = bf16[512,2048]{1,0:T(8,128)(2,1)} fusion(bf16[4096,2048]{1,0:T(8,128)(2,1)} %all-gather.12.cloned.1.call-done, bf16[512,4096]{1,0:T(8,128)(2,1)} %param.11, f32[4096]{0:T(1024)S(1)} %bitcast.128, f32[512]{0:T(512)S(1)} %add_rsqrt_fusion, f32[512]{0:T(512)S(1)} %broadcast_multiply_fusion.1), kind=kOutput, calls=%fused_computation.32 | convolution fusion | flops 8668577792 | bytes 23089152 | tf_op jit(solution)/shard_map/dot_general | solution.py:74
  568.5 253.4 %all-reduce.8.cloned.1.call-done = (f32[2,32,256,128]{3,2,1,0:T(8,128)}, f32[2,32,256]{2,1,0:T(8,128)}) async-done(((f32[2,32,256,128]{3,2,1,0:T(8,128)}, f32[2,32,256]{2,1,0:T(8,128)}), (f32[2,32,256,128]{3,2,1,0:T(8,128)}, f32[2,32,256]{2,1,0:T(8,128)})) %all-reduce.8.cloned.1.call-update) | async-done | bytes 8454160
  822.6 2.4 fusion.34
  825.4 31.5 %all-gather.10.cloned.1.call-done = bf16[512,4096]{1,0:T(8,128)(2,1)} async-done(((bf16[512,1024]{1,0:T(8,128)(2,1)}), bf16[512,4096]{1,0:T(8,128)(2,1)}) %all-gather.10.cloned.1.call-update) | async-done | bytes 4194320 | tf_op jit(solution)/shard_map/all_gather | solution.py:153
  856.9 8.0 fusion.35
  864.9 99.6 %all-gather.14.cloned.1.call-done = bf16[2048,4096]{1,0:T(8,128)(2,1)} async-done(((bf16[2048,1024]{1,0:T(8,128)(2,1)}), bf16[2048,4096]{1,0:T(8,128)(2,1)}) %all-gather.14.cloned.1.call-update) | async-done | bytes 16777232 | tf_op jit(solution)/shard_map/all_gather | solution.py:154
  964.5 15.6 %convolution_add_fusion = f32[512,4096]{1,0:T(8,128)} fusion(f32[512,4096]{1,0:T(8,128)} %fusion.35, bf16[512,2048]{1,0:T(8,128)(2,1)S(1)} %copy-done.9, bf16[2048,4096]{1,0:T(8,128)(2,1)} %all-gather.14.cloned.1.call-done), kind=kOutput, calls=%fused_computation.28 | convolution fusion | flops 8592031744 | bytes 35651584 | tf_op jit(solution)/shard_map/dot_general | solution.py:155
  980.1 6.5 convert_element_type.59
  986.6 143.1 %reduce-scatter.6.cloned.1.call-done = f32[512,512]{1,0:T(8,128)} async-done(((f32[512,4096]{1,0:T(8,128)}), f32[512,512]{1,0:T(8,128)}) %reduce-scatter.6.cloned.1.call-update) | async-done | bytes 1048592 | tf_op jit(solution)/shard_map/reduce_scatter | solution.py:158
  1129.7 2.7 dynamic-slice_add_fusion
  (166 shorter events, 59.3 us)
Async XLA Ops:
  6.5 89.7 %all-gather.6.cloned.1.call-start = ((), (), s32[]{:S(2)}) async-start(), calls=%async_computation.1 | async-start | bytes 15728640 | tf_op jit(solution)/shard_map/all_gather | solution.py:68
  6.5 4.8 copy-start.7
  11.3 173.9 %all-gather.8.cloned.1.call-start = ((), (), s32[]{:S(2)}) async-start(), calls=%async_computation.2 | async-start | bytes 4718592 | tf_op jit(solution)/shard_map/all_gather | solution.py:94
  11.3 3.5 copy-start.2
  11.4 4.8 copy-start.5
  107.3 1.6 copy-start.3
  107.3 2.9 copy-start.6
  110.0 328.0 %all-reduce.6.cloned.1.call-start = ((), (), s32[]{:S(2)}) async-start(), calls=%async_computation.3 | async-start | bytes 131072 | tf_op jit(solution)/shard_map/pmax | solution.py:140
  199.9 7.2 copy-start.1
  209.4 6.4 copy-start
  221.8 7.2 copy-start.1
  231.4 6.4 copy-start
  243.8 7.2 copy-start.1
  253.3 6.4 copy-start
  265.7 7.2 copy-start.1
  275.2 6.4 copy-start
  287.7 7.2 copy-start.1
  297.2 6.4 copy-start
  309.6 7.2 copy-start.1
  319.1 6.4 copy-start
  331.5 7.2 copy-start.1
  341.0 6.4 copy-start
  353.5 7.2 copy-start.1
  363.0 6.4 copy-start
  370.4 0.6 copy-start.4
  371.0 174.3 %all-gather.12.cloned.1.call-start = ((), (), s32[]{:S(2)}) async-start(), calls=%async_computation.5 | async-start | bytes 20971520 | tf_op jit(solution)/shard_map/all_gather | solution.py:69
  371.6 450.2 %all-reduce.8.cloned.1.call-start = ((), (), s32[]{:S(2)}) async-start(), calls=%async_computation.8 | async-start | bytes 16908288
  447.5 1.6 copy-start.8
  447.5 409.4 %all-gather.10.cloned.1.call-start = ((), (), s32[]{:S(2)}) async-start(), calls=%async_computation.4 | async-start | bytes 5242880 | tf_op jit(solution)/shard_map/all_gather | solution.py:153
  448.1 516.4 %all-gather.14.cloned.1.call-start = ((), (), s32[]{:S(2)}) async-start(), calls=%async_computation.6 | async-start | bytes 20971520 | tf_op jit(solution)/shard_map/all_gather | solution.py:154
  448.8 680.9 %reduce-scatter.6.cloned.1.call-start = ((), (), s32[]{:S(2)}) async-start(), calls=%async_computation.7 | async-start | bytes 9437184 | tf_op jit(solution)/shard_map/reduce_scatter | solution.py:158
  856.9 107.6 %copy-start.9 = (bf16[512,2048]{1,0:T(8,128)(2,1)S(1)}, bf16[512,2048]{1,0:T(8,128)(2,1)}, u32[]{:S(2)}) copy-start(bf16[512,2048]{1,0:T(8,128)(2,1)} %fusion.12) | copy-start | bytes 6291460
Sparse Core Ops, SparseCore 0:
  11.4 84.7 all-gather.5
  110.1 75.0 all-gather.7
  371.1 66.7 all-reduce.5
  439.4 105.8 all-gather.11
  549.7 272.0 all-reduce.7
  823.3 33.5 all-gather.9
  858.5 105.9 all-gather.13
  980.3 149.3 reduce-scatter.5
where the time goes:
time: 1140 us
  waiting for transfers between devices  834 us (73%)
  matrix products  155 us (14%)
  local copies, waits for them, and re-layouts  75.6 us (7%)
  other arithmetic  38 us (3%)
  loops' own time  21.1 us (2%)
  between operations  14.5 us (1%)
    unnamed x9, waiting for transfers between devices  255 us
    reduce_scatter x1, waiting for transfers between devices, per_device(): summed = lax.psum_scatter(value, 'kv', scatter_dimension=1, tiled=True)  143 us
    all_gather x1, waiting for transfers between devices, per_device(): down_piece = lax.all_gather(down_weight, 'req', axis=1, tiled=True)  99.6 us
    all_gather x1, waiting for transfers between devices, per_device(): up_piece = lax.all_gather(up_weight, 'req', axis=0, tiled=True)  92.6 us
    all_gather x1, waiting for transfers between devices, per_device(): qkv_piece = lax.all_gather(qkv_weight, 'req', axis=0, tiled=True)  80 us
    all_gather x1, waiting for transfers between devices, per_device(): lax.all_gather(query.reshape(rows, width_loc), 'kv', axis=1, tiled=True)  66.4 us
    pmax x1, waiting for transfers between devices, per_device(): largest = lax.pmax(with_new, 'kv')  66.3 us
    dot_general x8, matrix products, online_update(): jnp.einsum('hqk,hkd->hqd', weights, values, preferred_element_type=jnp.fl...  50.8 us
  transfers between devices with their start and end apart: 8, of which 8 were waited for; matrix products, arithmetic and copies ran while one was open for 6% of the time, Pallas kernels for 0%

commit v1 on v0

v1 whole, which is shorter than its diff:
```python
import functools

import jax
import jax.numpy as jnp
from jax import lax
from jax.experimental import pallas as pl
from jax.experimental.pallas import tpu as pltpu
from jax.sharding import PartitionSpec as P

D = 4096
HEADS = 32
HD = 128
ROT = 32
PAGE = 128
LOW = -1e30
FLOOR = -1e29


def layer_norm(x, gain):
    mean = jnp.mean(x, axis=-1, keepdims=True)
    cent = x - mean
    var = jnp.mean(cent * cent, axis=-1, keepdims=True)
    return cent * lax.rsqrt(var + 1e-05) * gain


def rotate(t, pos):
    half = ROT // 2
    freq = 10000.0 ** (-(jnp.arange(half, dtype=jnp.float32) * 2.0 / ROT))
    angle = pos[:, None] * freq[None, :]
    cosine = jnp.cos(angle)[:, None, :]
    sine = jnp.sin(angle)[:, None, :]
    first = t[..., :half]
    second = t[..., half:ROT]
    return jnp.concatenate(
        [first * cosine - second * sine, second * cosine + first * sine, t[..., ROT:]], axis=-1
    )


def exchange_kernel(n, views, n_arrays, *refs):
    srcs = refs[:n_arrays]
    dsts = refs[n_arrays : 2 * n_arrays]
    send_sem, recv_sem, local_sem = refs[2 * n_arrays :]
    me = lax.axis_index("kv")

    barrier = pltpu.get_barrier_semaphore()
    for off in range(1, n):
        pl.semaphore_signal(
            barrier,
            inc=1,
            device_id={"kv": lax.rem(me + off, n)},
            device_id_type=pl.DeviceIdType.MESH,
        )
    pl.semaphore_wait(barrier, n - 1)

    copies = []
    for off in range(n - 1, 0, -1):
        peer = lax.rem(me + off, n)
        for i in range(n_arrays):
            copy = pltpu.make_async_remote_copy(
                src_ref=views[i](srcs[i], peer),
                dst_ref=dsts[i].at[me],
                send_sem=send_sem.at[i, off],
                recv_sem=recv_sem.at[i, off],
                device_id={"kv": peer},
                device_id_type=pl.DeviceIdType.MESH,
            )
            copy.start()
            copies.append(copy)
    for i in range(n_arrays):
        own = pltpu.make_async_copy(views[i](srcs[i], me), dsts[i].at[me], local_sem.at[i])
        own.start()
        copies.append(own)
    for copy in copies:
        copy.wait()


def exchange(arrays, views, shapes, n, collective_id, cost_us):
    count = len(arrays)
    return pl.pallas_call(
        functools.partial(exchange_kernel, n, views, count),
        out_shape=[
            jax.ShapeDtypeStruct((n,) + shape, a.dtype) for shape, a in zip(shapes, arrays)
        ],
        in_specs=[pl.BlockSpec(memory_space=pl.ANY)] * count,
        out_specs=[pl.BlockSpec(memory_space=pl.ANY)] * count,
        scratch_shapes=[
            pltpu.SemaphoreType.DMA((count, n)),
            pltpu.SemaphoreType.DMA((count, n)),
            pltpu.SemaphoreType.DMA((count,)),
        ],
        compiler_params=pltpu.CompilerParams(collective_id=collective_id, has_side_effects=True),
        cost_estimate=pl.CostEstimate(
            flops=0, bytes_accessed=int(cost_us * 3.0e6), transcendentals=0
        ),
    )(*arrays)


def attention_kernel(
    groups, span, heads, slots, owner_ref, base_ref, len_ref, q_ref, cache_ref, acc_ref, stat_ref,
    s_scr, a_scr,
):
    scale = 1.0 / HD**0.5
    place = lax.broadcasted_iota(jnp.int32, (PAGE, span), 0)
    half = stat_ref.shape[2] // 2
    stat_ref[...] = jnp.zeros_like(stat_ref)
    for h in range(heads):
        tops = [jnp.full((1, span), FLOOR, jnp.float32) for _ in range(groups)]
        for s in range(slots):
            owner = owner_ref[s]
            q = q_ref[0, pl.ds(pl.multiple_of(owner * span, span), span), h * HD : (h + 1) * HD]
            st = lax.dot_general(
                cache_ref[s, 0, h], q, (((1,), (1,)), ((), ())), preferred_element_type=jnp.float32
            )
            st = jnp.where(place < len_ref[owner] - base_ref[s], st * scale, LOW)
            s_scr[s] = st
            col = jnp.max(st, axis=0, keepdims=True)
            tops = [jnp.maximum(t, jnp.where(owner == r, col, LOW)) for r, t in enumerate(tops)]
        sums = [jnp.zeros((1, span), jnp.float32) for _ in range(groups)]
        a_scr[...] = jnp.zeros_like(a_scr)
        for s in range(slots):
            owner = owner_ref[s]
            top = tops[0]
            for r in range(1, groups):
                top = jnp.where(owner == r, tops[r], top)
            p = jnp.exp(s_scr[s] - top).astype(jnp.bfloat16)
            part = jnp.sum(p.astype(jnp.float32), axis=0, keepdims=True)
            sums = [t + jnp.where(owner == r, part, 0.0) for r, t in enumerate(sums)]
            a_scr[owner] += lax.dot_general(
                cache_ref[s, 1, h], p, (((0,), (0,)), ((), ())), preferred_element_type=jnp.float32
            )
        for r in range(groups):
            acc_ref[0, r, h] = a_scr[r].astype(jnp.bfloat16)
            stat_ref[0, r, h : h + 1, :] = tops[r]
            stat_ref[0, r, half + h : half + h + 1, :] = sums[r]


def paged_attention(q_all, local_cache, owner_req, base, cached_len, groups, span, heads, half):
    n = q_all.shape[0]
    slots = local_cache.shape[0]
    rows, width = q_all.shape[1:]
    smem = pl.BlockSpec(memory_space=pltpu.SMEM)
    return pl.pallas_call(
        functools.partial(attention_kernel, groups, span, heads, slots),
        grid=(n,),
        out_shape=[
            jax.ShapeDtypeStruct((n, groups, heads, HD, span), jnp.bfloat16),
            jax.ShapeDtypeStruct((n, groups, 2 * half, span), jnp.float32),
        ],
        in_specs=[
            smem,
            smem,
            smem,
            pl.BlockSpec((1, rows, width), lambda j: (j, 0, 0)),
            pl.BlockSpec((slots, 2, heads, PAGE, HD), lambda j: (0, 0, j, 0, 0)),
        ],
        out_specs=[
            pl.BlockSpec((1, groups, heads, HD, span), lambda j: (j, 0, 0, 0, 0)),
            pl.BlockSpec((1, groups, 2 * half, span), lambda j: (j, 0, 0, 0)),
        ],
        scratch_shapes=[
            pltpu.VMEM((slots, PAGE, span), jnp.float32),
            pltpu.VMEM((groups, HD, span), jnp.float32),
        ],
        compiler_params=pltpu.CompilerParams(vmem_limit_bytes=32 * 1024 * 1024),
        cost_estimate=pl.CostEstimate(
            flops=4 * slots * HEADS * span * PAGE * HD,
            bytes_accessed=60_000_000,
            transcendentals=slots * HEADS * span * PAGE,
        ),
    )(owner_req, base, cached_len, q_all, local_cache)


def after(x, y):
    return lax.optimization_barrier((x, y))[0]


def per_device(
    hidden_in,
    ln_gains,
    qkv_weight,
    dense_weight,
    up_weight,
    down_weight,
    cache,
    cached_len,
    page_table,
):
    n_kv = lax.axis_size("kv")
    me_kv = lax.axis_index("kv")
    rows = hidden_in.shape[0]
    groups_here = cached_len.shape[0]
    span_rows = rows // groups_here
    width_loc = qkv_weight.shape[2]
    heads_loc = width_loc // HD
    half = max(4, heads_loc)
    scale = 1.0 / HD**0.5
    x = hidden_in.astype(jnp.float32)
    h1 = layer_norm(x, ln_gains[0]).astype(jnp.bfloat16)
    h2 = layer_norm(x, ln_gains[1]).astype(jnp.bfloat16)
    qkv_piece = lax.all_gather(qkv_weight, "req", axis=0, tiled=True)
    up_piece = lax.all_gather(after(up_weight, qkv_piece), "req", axis=0, tiled=True)
    dense_piece = lax.all_gather(after(dense_weight, up_piece), "req", axis=1, tiled=True)
    down_piece = lax.all_gather(after(down_weight, dense_piece), "req", axis=1, tiled=True)
    count = qkv_piece.shape[0]
    qkv = jnp.dot(
        h1, qkv_piece.reshape(count, 3 * width_loc), preferred_element_type=jnp.float32
    )
    qkv = qkv.reshape(rows, 3, heads_loc, HD)
    offsets = jnp.arange(span_rows, dtype=jnp.int32)
    pos = (cached_len[:, None] + offsets[None, :]).reshape(rows).astype(jnp.float32)
    query = rotate(qkv[:, 0], pos).astype(jnp.bfloat16)
    key_new = rotate(qkv[:, 1], pos).astype(jnp.bfloat16)
    value_new = qkv[:, 2].astype(jnp.bfloat16)

    whole = lambda ref, peer: ref
    block = lambda ref, peer: ref.at[peer]
    (q_all,) = exchange(
        [query.reshape(rows, width_loc)], [whole], [(rows, width_loc)], n_kv, 1, 80
    )

    local_cache = cache[0]
    slots_here = local_cache.shape[0]
    slot_ids = me_kv * slots_here + jnp.arange(slots_here, dtype=jnp.int32)
    match = (page_table[None, :, :] == slot_ids[:, None, None]).astype(jnp.int32)
    owner_req = jnp.sum(
        match * jnp.arange(groups_here, dtype=jnp.int32)[None, :, None], axis=(1, 2)
    )
    owner_page = jnp.sum(
        match * jnp.arange(page_table.shape[1], dtype=jnp.int32)[None, None, :], axis=(1, 2)
    )
    acc, stat = paged_attention(
        q_all,
        local_cache,
        owner_req,
        owner_page * PAGE,
        cached_len,
        groups_here,
        span_rows,
        heads_loc,
        half,
    )
    acc_in, stat_in = exchange(
        [acc, stat], [block, block], [acc.shape[1:], stat.shape[1:]], n_kv, 2, 80
    )

    q_grp = query.reshape(groups_here, span_rows, heads_loc, HD)
    k_grp = key_new.reshape(groups_here, span_rows, heads_loc, HD)
    v_grp = value_new.reshape(groups_here, span_rows, heads_loc, HD)
    causal = (offsets[None, :] <= offsets[:, None])[None, None]
    s_new = jnp.einsum("gqhd,gkhd->ghqk", q_grp, k_grp, preferred_element_type=jnp.float32) * scale
    s_new = jnp.where(causal, s_new, LOW)
    top_new = jnp.max(s_new, axis=-1)
    p_new = jnp.where(causal, jnp.exp(s_new - top_new[..., None]), 0.0).astype(jnp.bfloat16)
    total_new = jnp.sum(p_new.astype(jnp.float32), axis=-1)
    accum_new = jnp.einsum("ghqk,gkhd->ghdq", p_new, v_grp, preferred_element_type=jnp.float32)

    tops = stat_in[:, :, :heads_loc, :]
    totals = stat_in[:, :, half : half + heads_loc, :]
    largest = jnp.maximum(jnp.max(tops, axis=0), top_new)
    factor = jnp.exp(tops - largest[None])
    fresh = jnp.exp(top_new - largest)
    denom = jnp.sum(totals * factor, axis=0) + total_new * fresh
    numer = jnp.sum(acc_in.astype(jnp.float32) * factor[:, :, :, None, :], axis=0)
    numer = numer + accum_new * fresh[:, :, None, :]
    att = (numer / denom[:, :, None, :]).astype(jnp.bfloat16)
    att = jnp.transpose(att, (0, 3, 1, 2)).reshape(rows, width_loc)

    up_acc = jnp.dot(h2, up_piece, preferred_element_type=jnp.float32)
    hidden = jax.nn.gelu(up_acc, approximate=False).astype(jnp.bfloat16)
    value = jnp.dot(att, dense_piece, preferred_element_type=jnp.float32) + jnp.dot(
        hidden, down_piece, preferred_element_type=jnp.float32
    )
    width_out = D // n_kv
    strip = lambda ref, peer: ref.at[
        :, pl.ds(pl.multiple_of(peer * width_out, width_out), width_out)
    ]
    (parts,) = exchange(
        [value.astype(jnp.bfloat16)], [strip], [(rows, width_out)], n_kv, 3, 80
    )
    residual = lax.dynamic_slice_in_dim(hidden_in, me_kv * width_out, width_out, 1)
    return residual.astype(jnp.float32) + jnp.sum(parts.astype(jnp.float32), axis=0)


def solution(mesh):
    placed = (
        P("req", None),
        P(),
        P("req", None, "kv"),
        P("kv", "req"),
        P("req", "kv"),
        P("kv", "req"),
        P("req", "kv", None, None, None, None),
        P("req"),
        P("req", None),
    )
    return jax.shard_map(
        per_device, mesh=mesh, in_specs=placed, out_specs=P("req", "kv"), check_vma=False
    )
```

time: 1140 us -> 644 us (0.56)
  waiting for transfers between devices: 834 us -> 228 us
  Pallas kernels: 0 us -> 310 us
  matrix products: 155 us -> 58.3 us
  local copies, waits for them, and re-layouts: 75.6 us -> 18.1 us
  other arithmetic: 38 us -> 14.4 us
  loops' own time: 21.1 us -> 0 us
    pallas_call x0 -> x4, Pallas kernels: none -> 310 us  [the longest x3 286 us: exchange(): pl.pallas_call(functools.partial(exchange_kernel, n, views, count), out_s...]
    unnamed x9 -> x4, waiting for transfers between devices: 255 us -> 0.07 us
    all_gather x4 -> x3, waiting for transfers between devices: 290 us -> 143 us  [the longest x1 107 us: per_device(): lax.all_gather(after(up_weight, qkv_piece), 'req', axis=0, tiled=True)]
    reduce_scatter x1 -> x0, waiting for transfers between devices: 143 us -> none  [per_device(): summed = lax.psum_scatter(value, 'kv', scatter_dimension=1, tiled=True)]
    dot_general x17 -> x1, matrix products: 94.1 us -> 0.69 us  [per_device(): jnp.einsum('ghqk,gkhd->ghdq', p_new, v_grp, preferred_element_type=jnp.fl...]
    pmax x1 -> x0, waiting for transfers between devices: 66.3 us -> none  [per_device(): largest = lax.pmax(with_new, 'kv')]
    dynamic_slice x40 -> x0, local copies, waits for them, and re-layouts: 49.5 us -> none  [the longest x8 18 us: visit(): lax.dynamic_index_in_dim(accums, req, 0, keepdims=False)]
    another operation x1 -> x0, loops' own time: 21.1 us -> none  [per_device(): tops, totals, accums = lax.fori_loop(0, slots_here, visit, empty)]
  transfers between devices with their start and end apart: 8 -> 4, of which waited for: 8 -> 3; matrix products, arithmetic and copies ran while one was open for 6% -> 9% of each run, Pallas kernels for 0% -> 34%
where the time goes in v1:
time: 644 us; the launch traced here: 643 us
  Pallas kernels  310 us (48%)
  waiting for transfers between devices  228 us (35%)
  matrix products  58.3 us (9%)
  local copies, waits for them, and re-layouts  18.1 us (3%)
  other arithmetic  14.4 us (2%)
  between operations  13.5 us (2%)
    pallas_call x3, Pallas kernels, exchange(): pl.pallas_call(functools.partial(exchange_kernel, n, views, count), out_s...  286 us
    all_gather x1, waiting for transfers between devices, per_device(): lax.all_gather(after(up_weight, qkv_piece), 'req', axis=0, tiled=True)  107 us
    all_gather x1, waiting for transfers between devices, per_device(): qkv_piece = lax.all_gather(qkv_weight, 'req', axis=0, tiled=True)  84.9 us
    all_gather x1, waiting for transfers between devices, per_device(): lax.all_gather(after(dense_weight, up_piece), 'req', axis=1, tiled=True)  36 us
    pallas_call x1, Pallas kernels, paged_attention(): pl.pallas_call(functools.partial(attention_kernel, groups, span, heads, s...  24 us
    dot_general x1, matrix products, per_device(): up_acc = jnp.dot(h2, up_piece, preferred_element_type=jnp.float32)  22.6 us
    dot_general x1, matrix products, per_device(): jnp.dot(hidden, down_piece, preferred_element_type=jnp.float32)  17 us
  transfers between devices with their start and end apart: 4, of which 3 were waited for; matrix products, arithmetic and copies ran while one was open for 9% of the time, Pallas kernels for 34%

profile of v1, /device:TPU:0, one launch (start us, length us, event | category | flops | bytes accessed | tf_op | source)
XLA Modules:
  0.0 643.3 jit_solution(12213548360887298385)
XLA Ops:
  6.5 4.6 copy.30
  11.2 0.0 all-gather.7.cloned.1.call-start
  11.3 84.9 %all-gather.5.cloned.1.call-done = bf16[4096,3,512]{0,2,1:T(8,128)(2,1)} async-done(((bf16[1024,3,512]{0,2,1:T(8,128)(2,1)}), bf16[4096,3,512]{0,2,1:T(8,128)(2,1)}) %all-gather.5.cloned.1.call-update) | async-done | bytes 12582928 | tf_op jit(solution)/shard_map/all_gather | solution.py:200
  96.2 107.4 %all-gather.7.cloned.1.call-done = bf16[4096,2048]{1,0:T(8,128)(2,1)} async-done(((bf16[1024,2048]{1,0:T(8,128)(2,1)}), bf16[4096,2048]{1,0:T(8,128)(2,1)}) %all-gather.7.cloned.1.call-update) | async-done | bytes 16777232 | tf_op jit(solution)/shard_map/all_gather | solution.py:201
  203.7 36.0 %all-gather.9.cloned.1.call-done = bf16[512,4096]{1,0:T(8,128)(2,1)} async-done(((bf16[512,1024]{1,0:T(8,128)(2,1)}), bf16[512,4096]{1,0:T(8,128)(2,1)}) %all-gather.9.cloned.1.call-update) | async-done | bytes 4194320 | tf_op jit(solution)/shard_map/all_gather | solution.py:202
  239.8 0.1 convert_bitcast_fusion
  239.9 0.2 fusion.51
  240.1 0.6 iota_compare_fusion
  240.7 3.2 convert_reduce_fusion
  244.0 1.2 fusion.6
  245.2 0.2 multiply_cosine_fusion
  245.5 0.6 fusion.56
  246.1 11.1 %fusion.13 = f32[512,3,4,128]{0,3,2,1:T(8,128)S(1)} fusion(bf16[3,4,128,4096]{3,2,1,0:T(8,128)(2,1)} %bitcast.77, bf16[512,4096]{1,0:T(8,128)(2,1)S(1)} %copy-done.4, f32[4096]{0:T(1024)S(1)} %bitcast.75, f32[512]{0:T(512)S(1)} %add_rsqrt_fusion, f32[512]{0:T(512)S(1)} %broadcast_multiply_fusion), kind=kOutput, calls=%fused_computation.18 | convolution fusion | flops 6452936704 | bytes 19943424 | tf_op jit(solution)/shard_map/dot_general | solution.py:205
  257.2 0.1 slice.79
  257.3 0.2 slice_bitcast_fusion
  257.5 0.1 slice.81
  257.5 0.1 slice.80
  257.6 0.1 subtract_convert_fusion
  257.7 0.3 copy.32
  258.0 0.3 copy.33
  258.4 1.0 copy.35
  259.4 1.0 copy.36
  260.4 0.1 concatenate.28
  260.5 0.5 copy.34
  261.0 0.8 concatenate.32
  261.8 1.3 copy.37
  263.2 0.9 pad_maximum_fusion
  264.1 1.0 copy.43.refs_0_
  265.1 96.0 %shard_map.91.q_ref = bf16[8,512,512]{2,1,0:T(8,128)(2,1)} custom-call(bf16[512,512]{1,0:T(8,128)(2,1)} %copy.43.refs_0_), custom_call_target="tpu_custom_call" | custom-call | bytes 240000000 | tf_op jit(solution)/shard_map/pallas_call | solution.py:79
  361.1 0.9 convert_element_type.65
  362.0 2.2 copy-done
  364.2 24.0 %shard_map.92 = (bf16[8,2,4,128,256]{4,3,2,1,0:T(8,128)(2,1)S(1)}, f32[8,2,8,256]{3,2,1,0:T(8,128)S(1)}) custom-call(s32[8]{0:T(128)S(1)} %get-tuple-element.20.owner_ref, s32[8]{0:T(128)S(1)} %broadcast_multiply_fusion.1.base_ref, s32[2]{0:T(128)S(1)} %copy-done.3, bf16[8,512,512]{2,1,0:T(8,128)(2,1)S(1)} %copy-done, bf16[8,2,32,128,128]{4,3,2,1,0:T(8,128)(2,1)} %bitcast.71), custom_call_target="tpu_custom_call" | custom-call | flops 4294967296 | bytes 60000000 | tf_op jit(solution)/shard_map/pallas_call | solution.py:142
  388.2 1.9 copy-done.1
  390.2 0.7 copy-done.2
  390.8 97.2 %shard_map.93 = (bf16[8,2,4,128,256]{4,3,2,1,0:T(8,128)(2,1)}, f32[8,2,8,256]{3,2,1,0:T(8,128)}) custom-call(bf16[8,2,4,128,256]{4,3,2,1,0:T(8,128)(2,1)} %copy-done.1, f32[8,2,8,256]{3,2,1,0:T(8,128)} %copy-done.2), custom_call_target="tpu_custom_call" | custom-call | bytes 240000000 | tf_op jit(solution)/shard_map/pallas_call | solution.py:79
  488.0 1.1 slice_reduce_fusion
  489.1 1.4 fusion.30
  490.5 0.1 multiply_reduce_fusion.1
  490.6 0.5 convert_reduce_fusion.2
  491.1 1.0 multiply_reduce_fusion
  492.2 0.7 fusion.34
  492.9 0.3 copy.40
  493.2 22.6 %fusion.9 = bf16[512,2048]{1,0:T(8,128)(2,1)S(1)} fusion(bf16[4096,2048]{1,0:T(8,128)(2,1)} %all-gather.7.cloned.1.call-done, bf16[512,4096]{1,0:T(8,128)(2,1)} %param.9, f32[4096]{0:T(1024)S(1)} %bitcast.74, f32[512]{0:T(512)S(1)} %copy-done.17, f32[512]{0:T(512)S(1)} %broadcast_multiply_fusion), kind=kOutput, calls=%fused_computation.15 | convolution fusion | flops 8668577792 | bytes 23089152 | tf_op jit(solution)/shard_map/dot_general | solution.py:268
  515.8 5.6 fusion.35
  521.4 17.0 %add_convert_fusion.refs_0_ = bf16[512,4096]{1,0:T(8,128)(2,1)} fusion(f32[512,4096]{1,0:T(8,128)} %fusion.35, bf16[512,2048]{1,0:T(8,128)(2,1)S(1)} %fusion.9, bf16[2048,4096]{1,0:T(8,128)(2,1)} %all-gather.11.cloned.1.call-done), kind=kOutput, calls=%fused_computation.10 | convolution fusion | flops 8594128896 | bytes 31457280 | tf_op jit(solution)/shard_map/dot_general | solution.py:270
  538.4 93.3 %shard_map.94 = bf16[8,512,512]{2,1,0:T(8,128)(2,1)} custom-call(bf16[512,4096]{1,0:T(8,128)(2,1)} %add_convert_fusion.refs_0_), custom_call_target="tpu_custom_call" | custom-call | bytes 240000000 | tf_op jit(solution)/shard_map/pallas_call | solution.py:79
  631.6 2.9 convert_reduce_fusion.1
  634.5 2.2 convert_add_fusion
  (55 shorter events, 0.4 us)
Async XLA Ops:
  6.5 89.6 %all-gather.5.cloned.1.call-start = ((), (), s32[]{:S(2)}) async-start(), calls=%async_computation | async-start | bytes 15728640 | tf_op jit(solution)/shard_map/all_gather | solution.py:200
  11.2 228.6 %copy-start.3 = (s32[2]{0:T(128)S(1)}, s32[2]{0:T(128)}, u32[]{:S(2)}) copy-start(s32[2]{0:T(128)} %len_ref.1) | copy-start | bytes 28
  11.2 228.7 %copy-start.18 = (s32[2,32]{1,0:T(2,128)S(1)}, s32[2,32]{1,0:T(2,128)}, u32[]{:S(2)}) copy-start(s32[2,32]{1,0:T(2,128)} %param.17) | copy-start | bytes 772
  11.2 192.4 %all-gather.7.cloned.1.call-start = ((), (), s32[]{:S(2)}) async-start(), calls=%async_computation.1 | async-start | bytes 20971520 | tf_op jit(solution)/shard_map/all_gather | solution.py:201
  96.2 143.6 %all-gather.9.cloned.1.call-start = ((), (), s32[]{:S(2)}) async-start(), calls=%async_computation.2 | async-start | bytes 5242880 | tf_op jit(solution)/shard_map/all_gather | solution.py:202
  203.7 317.7 %all-gather.11.cloned.1.call-start = ((), (), s32[]{:S(2)}) async-start(), calls=%async_computation.3 | async-start | bytes 20971520 | tf_op jit(solution)/shard_map/all_gather | solution.py:203
  239.9 4.1 copy-start.4
  240.7 4.7 copy-start.14
  245.2 12.0 %copy-start.16 = (f32[512]{0:T(512)}, f32[512]{0:T(512)S(1)}, u32[]{:S(2)}) copy-start(f32[512]{0:T(512)S(1)} %add_rsqrt_fusion) | copy-start | bytes 6148
  257.7 4.2 copy-start.10
  257.7 4.2 copy-start.11
  362.0 2.2 copy-start
  388.2 2.0 copy-start.1
  390.1 0.7 copy-start.2
  390.8 98.3 %copy-start.7 = (bf16[2,256,4,16]{3,1,2,0:T(8,128)(2,1)S(1)}, bf16[2,256,4,16]{3,1,2,0:T(8,128)(2,1)}, u32[]{:S(2)}) copy-start(bf16[2,256,4,16]{3,1,2,0:T(8,128)(2,1)} %copy.35) | copy-start | bytes 196612
  390.8 98.3 %copy-start.8 = (bf16[2,256,4,16]{3,1,2,0:T(8,128)(2,1)S(1)}, bf16[2,256,4,16]{3,1,2,0:T(8,128)(2,1)}, u32[]{:S(2)}) copy-start(bf16[2,256,4,16]{3,1,2,0:T(8,128)(2,1)} %copy.36) | copy-start | bytes 196612
  390.8 98.3 %copy-start.9 = (pred[256,256]{0,1:T(8,128)(4,1)S(1)}, pred[256,256]{0,1:T(8,128)(4,1)}, u32[]{:S(2)}) copy-start(pred[256,256]{0,1:T(8,128)(4,1)} %iota_compare_fusion) | copy-start | bytes 196612
  488.0 2.5 copy-start.13
  488.0 3.1 copy-start.6
  490.5 1.7 copy-start.12
  492.2 1.0 copy-start.15
  492.2 1.0 copy-start.17
  493.2 22.6 %copy-start.5 = (bf16[512,4096]{1,0:T(8,128)(2,1)S(1)}, bf16[512,4096]{1,0:T(8,128)(2,1)}, u32[]{:S(2)}) copy-start(bf16[512,4096]{1,0:T(8,128)(2,1)} %all-gather.9.cloned.1.call-done) | copy-start | bytes 12582916
Sparse Core Ops, SparseCore 0:
  11.3 84.7 all-gather.4
  97.7 105.9 all-gather.6
  205.2 34.4 all-gather.8
  241.2 105.9 all-gather.10

commit v2 on v1

--- a/solution.py
+++ b/solution.py
@@ -93,6 +93,137 @@
             flops=0, bytes_accessed=int(cost_us * 3.0e6), transcendentals=0
         ),
     )(*arrays)
+
+
+def pair_entry(n):
+    me = lax.axis_index("kv")
+    par = lax.rem(me, 2)
+    idx = me // 2
+    partner = me + 1 - 2 * par
+    half = n // 2
+    barrier = pltpu.get_barrier_semaphore()
+    for t in range(half):
+        peer = partner if t == half - 1 else 2 * lax.rem(idx + 1 + t, half) + par
+        pl.semaphore_signal(
+            barrier, inc=1, device_id={"kv": peer}, device_id_type=pl.DeviceIdType.MESH
+        )
+    pl.semaphore_wait(barrier, half)
+    return idx, par, partner
+
+
+def send(src, dst, send_sem, recv_sem, peer):
+    copy = pltpu.make_async_remote_copy(
+        src_ref=src,
+        dst_ref=dst,
+        send_sem=send_sem,
+        recv_sem=recv_sem,
+        device_id={"kv": peer},
+        device_id_type=pl.DeviceIdType.MESH,
+    )
+    copy.start()
+    return copy
+
+
+def gather_kernel(n, src, dst, line_send, line_recv, pair_send, pair_recv, local_sem):
+    idx, par, partner = pair_entry(n)
+    me = lax.axis_index("kv")
+    half = n // 2
+    line = []
+    for t in range(half - 1):
+        peer = 2 * lax.rem(idx + 1 + t, half) + par
+        line.append(send(src, dst.at[me], line_send.at[t], line_recv.at[t], peer))
+    pair = [send(src, dst.at[me], pair_send.at[half - 1], pair_recv.at[half - 1], partner)]
+    own = pltpu.make_async_copy(src, dst.at[me], local_sem)
+    own.start()
+    for t in range(half - 1):
+        line[t].wait_recv()
+        origin = 2 * lax.rem(idx - 1 - t + half, half) + par
+        pair.append(
+            send(dst.at[origin], dst.at[origin], pair_send.at[t], pair_recv.at[t], partner)
+        )
+    for copy in line:
+        copy.wait_send()
+    for copy in pair:
+        copy.wait()
+    own.wait()
+
+
+def gather_queries(query, n, collective_id):
+    half = n // 2
+    return pl.pallas_call(
+        functools.partial(gather_kernel, n),
+        out_shape=jax.ShapeDtypeStruct((n,) + query.shape, query.dtype),
+        in_specs=[pl.BlockSpec(memory_space=pl.ANY)],
+        out_specs=pl.BlockSpec(memory_space=pl.ANY),
+        scratch_shapes=[pltpu.SemaphoreType.DMA((half,))] * 4 + [pltpu.SemaphoreType.DMA],
+        compiler_params=pltpu.CompilerParams(collective_id=collective_id, has_side_effects=True),
+        cost_estimate=pl.CostEstimate(flops=0, bytes_accessed=200_000_000, transcendentals=0),
+    )(query)
+
+
+def reduce_kernel(
+    n, value, residual, out, pair_buf, sum_buf, line_buf, line_send, line_recv, pair_send, pair_recv
+):
+    idx, par, partner = pair_entry(n)
+    half = n // 2
+    rows, width = out.shape
+    step = 64
+    pair = []
+    line = []
+    for t in range(half):
+        first = (2 * lax.rem(idx + 1 + t, half) + 1 - par) * width
+        strip = value.at[:, pl.ds(pl.multiple_of(first, width), width)]
+        pair.append(send(strip, pair_buf.at[t], pair_send.at[t], pair_recv.at[t], partner))
+    for t in range(half):
+        peer = 2 * lax.rem(idx + 1 + t, half) + par
+        columns = pl.ds(pl.multiple_of(peer * width, width), width)
+        pair[t].wait_recv()
+
+        @pl.loop(0, rows // step)
+        def _(i):
+            some = pl.ds(pl.multiple_of(i * step, step), step)
+            both = value[some, columns].astype(jnp.float32) + pair_buf[t, some, :].astype(
+                jnp.float32
+            )
+            if t == half - 1:
+                out[some, :] = residual[some, :].astype(jnp.float32) + both
+            else:
+                sum_buf[t, some, :] = both.astype(jnp.bfloat16)
+
+        if t < half - 1:
+            line.append(
+                send(sum_buf.at[t], line_buf.at[t], line_send.at[t], line_recv.at[t], peer)
+            )
+    for t in range(half - 1):
+        line[t].wait_recv()
+
+        @pl.loop(0, rows // step)
+        def _(i):
+            some = pl.ds(pl.multiple_of(i * step, step), step)
+            out[some, :] += line_buf[t, some, :].astype(jnp.float32)
+
+    for copy in pair + line:
+        copy.wait_send()
+
+
+def reduce_output(value, residual, n, collective_id):
+    half = n // 2
+    rows, width = residual.shape
+    vmem = pl.BlockSpec(memory_space=pltpu.VMEM)
+    return pl.pallas_call(
+        functools.partial(reduce_kernel, n),
+        out_shape=jax.ShapeDtypeStruct((rows, width), jnp.float32),
+        in_specs=[vmem, vmem],
+        out_specs=vmem,
+        scratch_shapes=[pltpu.VMEM((half, rows, width), jnp.bfloat16)] * 3
+        + [pltpu.SemaphoreType.DMA((half,))] * 4,
+        compiler_params=pltpu.CompilerParams(
+            collective_id=collective_id,
+            has_side_effects=True,
+            vmem_limit_bytes=24 * 1024 * 1024,
+        ),
+        cost_estimate=pl.CostEstimate(flops=0, bytes_accessed=200_000_000, transcendentals=0),
+    )(value, residual)
 
 
 def attention_kernel(
@@ -199,8 +330,6 @@
     h2 = layer_norm(x, ln_gains[1]).astype(jnp.bfloat16)
     qkv_piece = lax.all_gather(qkv_weight, "req", axis=0, tiled=True)
     up_piece = lax.all_gather(after(up_weight, qkv_piece), "req", axis=0, tiled=True)
-    dense_piece = lax.all_gather(after(dense_weight, up_piece), "req", axis=1, tiled=True)
-    down_piece = lax.all_gather(after(down_weight, dense_piece), "req", axis=1, tiled=True)
     count = qkv_piece.shape[0]
     qkv = jnp.dot(
         h1, qkv_piece.reshape(count, 3 * width_loc), preferred_element_type=jnp.float32
@@ -212,12 +341,8 @@
     key_new = rotate(qkv[:, 1], pos).astype(jnp.bfloat16)
     value_new = qkv[:, 2].astype(jnp.bfloat16)
 
-    whole = lambda ref, peer: ref
+    q_all = gather_queries(query.reshape(rows, width_loc), n_kv, 1)
     block = lambda ref, peer: ref.at[peer]
-    (q_all,) = exchange(
-        [query.reshape(rows, width_loc)], [whole], [(rows, width_loc)], n_kv, 1, 80
-    )
-
     local_cache = cache[0]
     slots_here = local_cache.shape[0]
     slot_ids = me_kv * slots_here + jnp.arange(slots_here, dtype=jnp.int32)
@@ -239,6 +364,9 @@
         heads_loc,
         half,
     )
+    up_piece = after(up_piece, stat)
+    dense_piece = lax.all_gather(after(dense_weight, up_piece), "req", axis=1, tiled=True)
+    down_piece = lax.all_gather(after(down_weight, up_piece), "req", axis=1, tiled=True)
     acc_in, stat_in = exchange(
         [acc, stat], [block, block], [acc.shape[1:], stat.shape[1:]], n_kv, 2, 80
     )
@@ -271,14 +399,8 @@
         hidden, down_piece, preferred_element_type=jnp.float32
     )
     width_out = D // n_kv
-    strip = lambda ref, peer: ref.at[
-        :, pl.ds(pl.multiple_of(peer * width_out, width_out), width_out)
-    ]
-    (parts,) = exchange(
-        [value.astype(jnp.bfloat16)], [strip], [(rows, width_out)], n_kv, 3, 80
-    )
     residual = lax.dynamic_slice_in_dim(hidden_in, me_kv * width_out, width_out, 1)
-    return residual.astype(jnp.float32) + jnp.sum(parts.astype(jnp.float32), axis=0)
+    return reduce_output(value.astype(jnp.bfloat16), residual, n_kv, 3)
 
 
 def solution(mesh):

time: 644 us -> 442 us (0.69)
  waiting for transfers between devices: 228 us -> 85.3 us
  Pallas kernels: 310 us -> 254 us
    pallas_call x3 -> x1, Pallas kernels: 286 us -> 107 us  [exchange(): pl.pallas_call(functools.partial(exchange_kernel, n, views, count), out_s...]
    pallas_call x0 -> x2, Pallas kernels: none -> 123 us  [the longest x1 64.1 us: gather_queries(): pl.pallas_call(functools.partial(gather_kernel, n), out_shape=jax.ShapeDt...]
    all_gather x1, waiting for transfers between devices: 107 us -> 0.01 us  [per_device(): lax.all_gather(after(up_weight, qkv_piece), 'req', axis=0, tiled=True)]
    all_gather x1, waiting for transfers between devices: 36 us -> 0.02 us  [per_device(): lax.all_gather(after(dense_weight, up_piece), 'req', axis=1, tiled=True)]
  transfers between devices with their start and end apart: 4 -> 4, of which waited for: 3 -> 1; matrix products, arithmetic and copies ran while one was open for 9% -> 14% of each run, Pallas kernels for 34% -> 44%
where the time goes in v2:
time: 442 us
  Pallas kernels  254 us (57%)
  waiting for transfers between devices  85.3 us (19%)
  matrix products  57.9 us (13%)
  local copies, waits for them, and re-layouts  22.1 us (5%)
  between operations  13.5 us (3%)
  other arithmetic  9.16 us (2%)
    pallas_call x1, Pallas kernels, exchange(): pl.pallas_call(functools.partial(exchange_kernel, n, views, count), out_s...  107 us
    all_gather x1, waiting for transfers between devices, per_device(): qkv_piece = lax.all_gather(qkv_weight, 'req', axis=0, tiled=True)  84.9 us
    pallas_call x1, Pallas kernels, gather_queries(): pl.pallas_call(functools.partial(gather_kernel, n), out_shape=jax.ShapeDt...  64.1 us
    pallas_call x1, Pallas kernels, reduce_output(): pl.pallas_call(functools.partial(reduce_kernel, n), out_shape=jax.ShapeDt...  58.9 us
    pallas_call x1, Pallas kernels, paged_attention(): pl.pallas_call(functools.partial(attention_kernel, groups, span, heads, s...  23.6 us
    dot_general x1, matrix products, per_device(): up_acc = jnp.dot(h2, up_piece, preferred_element_type=jnp.float32)  22.6 us
    dot_general x1, matrix products, per_device(): jnp.dot(hidden, down_piece, preferred_element_type=jnp.float32)  13.6 us
    unnamed x35, local copies, waits for them, and re-layouts  11.8 us
  transfers between devices with their start and end apart: 4, of which 1 were waited for; matrix products, arithmetic and copies ran while one was open for 14% of the time, Pallas kernels for 44%

profile of v2, /device:TPU:0, one launch (start us, length us, event | category | flops | bytes accessed | tf_op | source)
XLA Modules:
  0.0 442.0 jit_solution(2080901184644875384)
XLA Ops:
  6.5 4.6 %copy.30 = bf16[1024,3,512]{0,2,1:T(8,128)(2,1)} copy(bf16[1024,3,512]{2,0,1:T(8,128)(2,1)} %param.11) | data formatting | bytes 6291456 | tf_op args[2]
  11.3 84.9 %all-gather.5.cloned.1.call-done = bf16[4096,3,512]{0,2,1:T(8,128)(2,1)} async-done(((bf16[1024,3,512]{0,2,1:T(8,128)(2,1)}), bf16[4096,3,512]{0,2,1:T(8,128)(2,1)}) %all-gather.5.cloned.1.call-update) | async-done | bytes 12582928 | tf_op jit(solution)/shard_map/all_gather | solution.py:331
  96.3 0.1 convert_bitcast_fusion
  96.4 0.2 fusion.51
  96.6 3.0 convert_reduce_fusion
  99.5 0.2 copy-done.4
  99.8 1.2 fusion.6
  101.0 0.2 multiply_cosine_fusion
  101.3 10.4 %fusion.13 = f32[512,3,4,128]{0,3,2,1:T(8,128)S(1)} fusion(bf16[3,4,128,4096]{3,2,1,0:T(8,128)(2,1)} %bitcast.77, bf16[512,4096]{1,0:T(8,128)(2,1)S(1)} %copy-done.4, f32[4096]{0:T(1024)S(1)} %bitcast.75, f32[512]{0:T(512)S(1)} %add_rsqrt_fusion, f32[512]{0:T(512)S(1)} %broadcast_multiply_fusion), kind=kOutput, calls=%fused_computation.17 | convolution fusion | flops 6452936704 | bytes 19943424 | tf_op jit(solution)/shard_map/dot_general | solution.py:334
  111.7 0.2 slice_bitcast_fusion
  111.9 0.1 slice.81
  112.0 1.0 subtract_convert_fusion
  113.0 0.9 copy-done.6
  113.9 1.0 copy.43.src
  114.9 64.1 %shard_map.91.q_ref = bf16[8,512,512]{2,1,0:T(8,128)(2,1)} custom-call(bf16[512,512]{1,0:T(8,128)(2,1)} %copy.43.src), custom_call_target="tpu_custom_call" | custom-call | bytes 200000000 | tf_op jit(solution)/shard_map/pallas_call | solution.py:153
  179.0 2.4 copy-done
  181.4 23.6 %shard_map.92 = (bf16[8,2,4,128,256]{4,3,2,1,0:T(8,128)(2,1)S(1)}, f32[8,2,8,256]{3,2,1,0:T(8,128)S(1)}) custom-call(s32[8]{0:T(128)S(1)} %get-tuple-element.22.owner_ref, s32[8]{0:T(128)S(1)} %broadcast_multiply_fusion.1.base_ref, s32[2]{0:T(128)S(1)} %copy-done.3, bf16[8,512,512]{2,1,0:T(8,128)(2,1)S(1)} %copy-done, bf16[8,2,32,128,128]{4,3,2,1,0:T(8,128)(2,1)} %bitcast.71), custom_call_target="tpu_custom_call" | custom-call | flops 4294967296 | bytes 60000000 | tf_op jit(solution)/shard_map/pallas_call | solution.py:273
  205.0 1.9 copy-done.1
  207.0 0.6 copy-done.2
  207.6 0.2 all-gather.11.cloned.1.call-start
  207.9 0.3 all-gather.11.cloned.1.call-update
  208.2 0.6 iota_compare_fusion
  208.9 1.1 constant_dynamic-slice_fusion.residual
  210.0 0.1 concatenate.28
  210.2 1.3 slice.79
  211.5 0.3 copy.32
  211.7 0.3 copy.33
  212.0 0.9 concatenate.30
  212.9 1.0 copy.35
  213.9 0.9 concatenate.31
  214.8 1.0 copy.36
  215.8 0.4 copy.34
  216.3 0.1 concatenate.32
  216.4 0.5 copy.37
  216.8 107.1 %shard_map.93 = (bf16[8,2,4,128,256]{4,3,2,1,0:T(8,128)(2,1)}, f32[8,2,8,256]{3,2,1,0:T(8,128)}) custom-call(bf16[8,2,4,128,256]{4,3,2,1,0:T(8,128)(2,1)} %copy-done.1, f32[8,2,8,256]{3,2,1,0:T(8,128)} %copy-done.2), custom_call_target="tpu_custom_call" | custom-call | bytes 240000000 | tf_op jit(solution)/shard_map/pallas_call | solution.py:79
  323.9 0.9 convert_element_type.58
  324.9 1.1 slice_reduce_fusion
  326.0 2.8 fusion.30
  328.8 0.1 multiply_reduce_fusion.1
  328.8 0.5 convert_reduce_fusion.1
  329.4 1.1 multiply_reduce_fusion
  330.5 0.7 fusion.34
  331.3 0.3 copy.40
  331.6 22.6 %fusion.9 = bf16[512,2048]{1,0:T(8,128)(2,1)S(1)} fusion(bf16[4096,2048]{1,0:T(8,128)(2,1)} %all-gather.7.cloned.1.call-done, bf16[512,4096]{1,0:T(8,128)(2,1)} %param.9, f32[4096]{0:T(1024)S(1)} %bitcast.74, f32[512]{0:T(512)S(1)} %copy-done.14, f32[512]{0:T(512)S(1)} %copy-done.12), kind=kOutput, calls=%fused_computation.14 | convolution fusion | flops 8668577792 | bytes 23089152 | tf_op jit(solution)/shard_map/dot_general | solution.py:396
  354.2 7.8 %fusion.35 = f32[512,4096]{1,0:T(8,128)} fusion(bf16[512,4096]{1,0:T(8,128)(2,1)} %all-gather.9.cloned.1.call-done, bf16[64,8,4,128]{3,2,1,0:T(4,128)(2,1)S(1)} %bitcast.72), kind=kOutput, calls=%fused_computation.53 | convolution fusion | flops 2147483648 | bytes 13107200 | tf_op jit(solution)/shard_map/dot_general | solution.py:398
  362.0 13.6 %add_convert_fusion.value = bf16[512,4096]{1,0:T(8,128)(2,1)S(1)} fusion(f32[512,4096]{1,0:T(8,128)} %fusion.35, bf16[512,2048]{1,0:T(8,128)(2,1)S(1)} %fusion.9, bf16[2048,4096]{1,0:T(8,128)(2,1)} %all-gather.11.cloned.1.call-done), kind=kOutput, calls=%fused_computation.9 | convolution fusion | flops 8594128896 | bytes 31457280 | tf_op jit(solution)/shard_map/dot_general | solution.py:398
  375.6 58.9 %shard_map.94 = f32[512,512]{1,0:T(8,128)S(1)} custom-call(bf16[512,4096]{1,0:T(8,128)(2,1)S(1)} %add_convert_fusion.value, bf16[512,512]{1,0:T(8,128)(2,1)S(1)} %constant_dynamic-slice_fusion.residual), custom_call_target="tpu_custom_call" | custom-call | bytes 200000000 | tf_op jit(solution)/shard_map/pallas_call | solution.py:213
  434.5 1.0 copy.53
  (49 shorter events, 0.4 us)
Async XLA Ops:
  6.5 89.6 %all-gather.5.cloned.1.call-start = ((), (), s32[]{:S(2)}) async-start(), calls=%async_computation | async-start | bytes 15728640 | tf_op jit(solution)/shard_map/all_gather | solution.py:331
  11.2 85.1 %copy-start.3 = (s32[2]{0:T(128)S(1)}, s32[2]{0:T(128)}, u32[]{:S(2)}) copy-start(s32[2]{0:T(128)} %len_ref.1) | copy-start | bytes 28
  11.2 85.2 %copy-start.15 = (s32[2,32]{1,0:T(2,128)S(1)}, s32[2,32]{1,0:T(2,128)}, u32[]{:S(2)}) copy-start(s32[2,32]{1,0:T(2,128)} %param.17) | copy-start | bytes 772
  11.2 196.4 %all-gather.7.cloned.1.call-start = ((), (), s32[]{:S(2)}) async-start(), calls=%async_computation.1 | async-start | bytes 20971520 | tf_op jit(solution)/shard_map/all_gather | solution.py:332
  96.2 258.0 %all-gather.9.cloned.1.call-start = ((), (), s32[]{:S(2)}) async-start(), calls=%async_computation.2 | async-start | bytes 5242880 | tf_op jit(solution)/shard_map/all_gather | solution.py:368
  96.3 3.4 copy-start.4
  96.6 4.7 %copy-start.10 = (f32[2,4096]{1,0:T(2,128)S(1)}, f32[2,4096]{1,0:T(2,128)}, u32[]{:S(2)}) copy-start(f32[2,4096]{1,0:T(2,128)} %param.10) | copy-start | bytes 98308
  99.8 11.9 %copy-start.11 = (f32[512]{0:T(512)}, f32[512]{0:T(512)S(1)}, u32[]{:S(2)}) copy-start(f32[512]{0:T(512)S(1)} %broadcast_multiply_fusion) | copy-start | bytes 6148
  101.0 10.7 %copy-start.13 = (f32[512]{0:T(512)}, f32[512]{0:T(512)S(1)}, u32[]{:S(2)}) copy-start(f32[512]{0:T(512)S(1)} %add_rsqrt_fusion) | copy-start | bytes 6148
  111.7 2.2 copy-start.6
  179.0 2.4 copy-start
  205.0 2.0 copy-start.1
  207.0 0.6 copy-start.2
  207.6 154.3 %all-gather.11.cloned.1.call-start = ((), (), s32[]{:S(2)}) async-start(), calls=%async_computation.3 | async-start | bytes 20971520 | tf_op jit(solution)/shard_map/all_gather | solution.py:369
  216.8 109.1 %copy-start.7 = (pred[256,256]{0,1:T(8,128)(4,1)S(1)}, pred[256,256]{0,1:T(8,128)(4,1)}, u32[]{:S(2)}) copy-start(pred[256,256]{0,1:T(8,128)(4,1)} %iota_compare_fusion) | copy-start | bytes 196612
  323.9 4.8 %copy-start.9 = (f32[8,2,8,256]{3,2,1,0:T(8,128)S(1)}, f32[8,2,8,256]{3,2,1,0:T(8,128)}, u32[]{:S(2)}) copy-start(f32[8,2,8,256]{3,2,1,0:T(8,128)} %get-tuple-element.16) | copy-start | bytes 393220
  324.9 4.5 %copy-start.5 = (bf16[8,2,4,128,256]{4,3,2,1,0:T(8,128)(2,1)S(1)}, bf16[8,2,4,128,256]{4,3,2,1,0:T(8,128)(2,1)}, u32[]{:S(2)}) copy-start(bf16[8,2,4,128,256]{4,3,2,1,0:T(8,128)(2,1)} %get-tuple-element.15) | copy-start | bytes 12582916
  328.8 1.8 copy-start.8
  330.5 1.0 copy-start.12
  330.5 1.0 copy-start.14
Sparse Core Ops, SparseCore 0:
  11.3 84.7 all-gather.4
  97.7 105.9 all-gather.6
  207.8 43.1 all-gather.8
  252.4 105.9 all-gather.10
